TPU v7x, 128 devices: a whole 4x4x4 slice. The times are simulated.
128 devices in a mesh: circ: 8 (over z_lo, y), span: 16 (over z_hi, x, core).
Axes of the slice: x: 4, y: 4, z: 4 (z_hi: 2, z_lo: 2; z = z_hi * 2 + z_lo), core: 2. Of those that a mesh axis runs over, the one named last changes fastest.
Arguments:
- elem_rows: bfloat16 [80, 98304], P(None, ('circ', 'span')), may hold values from -6 to 6
- coupling: bfloat16 [48, 80, 80, 2048], P('circ', None, None, 'span')
- inverses: bfloat16 [48, 80, 80, 2048], P('circ', None, None, 'span'), may hold values from -0.625 to 0.625
- send_rows: int32 [128, 128, 12], P(('circ', 'span')), may hold values from 0 to 767, as said below
- recv_cells: int32 [128, 128, 12], P(('circ', 'span')), may hold values from 0 to 767, as said below
- slot_counts: int32 [128, 128], P(('circ', 'span')), may hold values from 0 to 12, as said below
Outputs:
- corrections: float32 [80, 98304], P(None, ('circ', 'span'))
Inputs may be any that keep to these rules, and one draw needn't show every extreme that they name: `send_rows`: each source's filled slots name each of its 768 rows exactly once, each owner's filled slots name each of its 768 cells exactly once; unfilled slots hold 0. `recv_cells`: as send_rows, for the owners' cells. `slot_counts`: every owner's counts sum to 768, and so do every source's; some pair fills all 12 slots.
All inputs are finite; a program needn't handle non-finite values.
Results may differ from a plain program's by a relative error of at most 0.0003.
Values may be sent and summed in bfloat16 or wider, within the bound.
No kernel may reach another device: no remote copies, remote signals or barrier semaphores. Data moves between devices by JAX's collectives and lax.ppermute only.
A program may use at most 128 MiB of HBM per device.

v0:
```python
import functools

import jax
import jax.numpy as jnp
from jax import lax
from jax.experimental import pallas as pl
from jax.experimental.pallas import tpu as pltpu
from jax.sharding import PartitionSpec as P

FEATURES = 80
SEGMENT = 6
LINES = 128
CELLS = SEGMENT * LINES
PEERS = 128
SLOTS = 12
PAIRS = SLOTS // 2
ROWS = 8
MAIN = 64
TAIL = FEATURES - MAIN
N_CIRC = 8
STEPS = 32000.0
SMALLEST = 2.0**-100
NEAR = 2
HALF = FEATURES // 2
LANES = 128
SIDE = LANES // 2

IN_VMEM = pl.BlockSpec(memory_space=pltpu.VMEM)
F32 = jnp.float32
BF16 = jnp.bfloat16


def params(megabytes):
    return pltpu.CompilerParams(vmem_limit_bytes=megabytes * 2**20)


def fold_sublanes(parts, row):
    upper = row < 4
    fours = []
    for k in range(4):
        a, b = parts[k], parts[k + 4]
        fours.append(jnp.where(upper, a, b) + pltpu.roll(jnp.where(upper, b, a), 4, 0))
    even_pair = (row & 2) == 0
    twos = []
    for k in range(2):
        a, b = fours[k], fours[k + 2]
        twos.append(jnp.where(even_pair, a + pltpu.roll(a, 6, 0), b + pltpu.roll(b, 2, 0)))
    even = (row & 1) == 0
    a, b = twos
    return jnp.where(even, a + pltpu.roll(a, 7, 0), b + pltpu.roll(b, 1, 0))


def matvec(blocks_ref, position, vector, row):
    result = []
    for group in range(blocks_ref.shape[1] // 8):
        parts = []
        for k in range(8):
            terms = blocks_ref[position, group * 8 + k].astype(F32) * vector
            total = terms[0:8]
            for j in (*range(16, FEATURES, 16), *range(8, FEATURES, 16)):
                total = total + terms[j : j + 8]
            parts.append(total)
        result.append(fold_sublanes(parts, row))
    return jnp.concatenate(result, axis=0)


def sublane_ids():
    return lax.broadcasted_iota(jnp.int32, (8, LINES), 0)


def columns(table):
    padded = jnp.concatenate([table, jnp.full((16 - SLOTS, PEERS), -1, jnp.int32)], axis=0)
    return jnp.transpose(padded)


def one_hot(index, first):
    place = lax.broadcasted_iota(jnp.int32, (PEERS, CELLS), 1)
    return jnp.concatenate(
        [
            jnp.where(index[:, 2 * pair + first : 2 * pair + first + 1] == place, 1.0, 0.0).astype(BF16)
            for pair in range(PAIRS)
        ],
        axis=0,
    )


def across(a, b):
    return lax.dot_general(a, b, (((1,), (1,)), ((), ())), preferred_element_type=F32)


def down(a, b):
    return lax.dot_general(a, b, (((0,), (0,)), ((), ())), preferred_element_type=F32)


def swap(x):
    return pltpu.roll(x, SIDE, 1)


def left(rows):
    return lax.broadcasted_iota(jnp.int32, (rows, LANES), 1) < SIDE


def spread(rows, odd, extra):
    parts = [jnp.zeros((MAIN, CELLS), BF16), jnp.zeros((TAIL, CELLS), BF16)]
    at = slice(None, None, -1) if odd else slice(None)
    main = [rows[:MAIN], parts[0]][at]
    tail = [rows[MAIN:], parts[1]][at]
    if extra is None:
        note = parts[1]
    else:
        place = lax.broadcasted_iota(jnp.int32, (TAIL, CELLS), 0)
        note = jnp.where(place == odd, extra, 0.0).astype(BF16)
    rest = jnp.zeros((128 - 3 * TAIL, CELLS), BF16)
    return jnp.concatenate([*main, *tail, note, rest], axis=0)


def pack(pieces, hots, store, extra=None):
    packed = 0.0
    for odd, hot in enumerate(hots):
        for k, piece in enumerate(pieces):
            packed = packed + across(hot, spread(piece, odd, None if k else extra))
    lane = lax.broadcasted_iota(jnp.int32, (PEERS, LANES), 1)
    tails = []
    notes = 0.0
    for pair in range(PAIRS):
        rows = packed[pair * PEERS : (pair + 1) * PEERS]
        store(pair, rows[:, :128])
        tail = rows[:, 128:]
        if extra is not None:
            notes = notes + pltpu.roll(jnp.where(lane < 2 * TAIL, 0.0, tail), 2 * TAIL + 2 * pair, 1)
            tail = jnp.where(lane < 2 * TAIL, tail, 0.0)
        shift = 2 * TAIL * (pair % 4)
        tails.append(pltpu.roll(tail, shift, 1) if shift else tail)
    store(6, tails[0] + tails[1] + tails[2] + tails[3])
    store(7, tails[4] + tails[5] + notes)


def unpack(load, hots, pieces, noted=False):
    lane = lax.broadcasted_iota(jnp.int32, (PEERS, LANES), 1)
    last = (load(6), load(7))
    total = 0.0
    for odd in range(2):
        slots = []
        for pair in range(PAIRS):
            rows = load(pair)
            if odd:
                rows = pltpu.roll(rows, MAIN, 1)
            shift = (MAIN - 2 * TAIL * (pair % 4) - TAIL * odd) % LANES
            tail = last[pair // 4]
            tail = pltpu.roll(tail, shift, 1) if shift else tail
            note = 0.0
            if noted:
                note = pltpu.roll(last[1], FEATURES - MAIN - 2 * pair - odd, 1)
                note = jnp.where(lane == FEATURES, note, 0.0)
            slots.append(jnp.where(lane < MAIN, rows, jnp.where(lane < FEATURES, tail, note)))
        slots = jnp.concatenate(slots, axis=0)
        hot = hots[odd]
        for _ in range(pieces):
            part = slots.astype(BF16)
            total = total + down(part, hot)
            slots = slots - part.astype(F32)
    if noted:
        return total[:FEATURES], total[FEATURES : FEATURES + 8]
    return total[:FEATURES]


def pack_rows_kernel(rows_hbm, send_ref, out_ref, wide, rows_ref, sem):
    copy = pltpu.make_async_copy(rows_hbm, rows_ref, sem)
    copy.start()

    def store(r, block):
        wide[pl.ds(r, PEERS, stride=ROWS), :] = block

    index = columns(send_ref[...].reshape(SLOTS, PEERS))
    hots = one_hot(index, 0), one_hot(index, 1)
    copy.wait()
    pack([rows_ref[...]], hots, store)
    out_ref[...] = wide[...].astype(BF16)


def bundle_kernel(
    coupling_hbm, inverses_hbm, bundle_a_hbm, bundle_b_hbm, near_ref,
    whole, bundle_a, bundle_b, sems, near_sem,
):
    fetch, put_a, put_b = [
        [pltpu.make_async_copy(src.at[p], dst.at[p], sems.at[k, p]) for p in range(SEGMENT)]
        for k, (src, dst) in enumerate(
            ((coupling_hbm, whole), (bundle_a, bundle_a_hbm), (bundle_b, bundle_b_hbm))
        )
    ]
    for copy in fetch:
        copy.start()
    near = pltpu.make_async_copy(inverses_hbm.at[pl.ds(0, NEAR)], near_ref, near_sem)
    near.start()
    on_left = left(FEATURES)
    for p in range(SEGMENT):
        fetch[p].wait()

        @pl.loop(0, HALF // 8)
        def _(block):
            for k in range(8):
                low = whole[p, block * 16 + k]
                high = whole[p, block * 16 + 8 + k].astype(F32)
                high = jnp.concatenate(
                    [swap(high[j * 8 : j * 8 + 8]) for i in range(HALF // 8) for j in (2 * i + 1, 2 * i)],
                    axis=0,
                ).astype(BF16)
                bundle_a[p, block * 8 + k] = jnp.where(on_left, low, high)
                bundle_b[p, block * 8 + k] = jnp.where(on_left, high, low)

        put_a[p].start()
        put_b[p].start()
    for copy in put_a + put_b:
        copy.wait()
    near.wait()


def blocks8(x, odd):
    return jnp.concatenate([x[j * 8 : j * 8 + 8] for j in range(odd, FEATURES // 8, 2)], axis=0)


def move(coupling_ref, at, forcing, state):
    own = [state[j : j + 8] for j in range(0, HALF, 8)]
    both = jnp.concatenate([x for block in own for x in (block, swap(block))], axis=0)
    return forcing + matvec(coupling_ref, at, both, sublane_ids())


def advance(coupling_ref, forcing_ref, first, state, record=None):
    def step(position, state):
        if callable(first):
            first(position)
        state = move(coupling_ref, position, forcing_ref[position], state)
        if record is not None:
            record[position] = state
        return state

    if callable(first):
        return lax.fori_loop(1, SEGMENT, step, state)
    return lax.fori_loop(first, SEGMENT, step, state, unroll=2 if first == 0 else True)


def forcing_kernel(
    arrived_ref, cells_ref, counts_ref, near_ref, inverses_hbm, bundle_hbm,
    forcing_a, forcing_b, bundle_ref, end_ref,
    wide, lines, inverses_ref, sems, bundle_sems,
):
    def copy(p):
        return pltpu.make_async_copy(inverses_hbm.at[p], inverses_ref.at[p], sems.at[p])

    def bundle_copy(p):
        return pltpu.make_async_copy(bundle_hbm.at[p], bundle_ref.at[p], bundle_sems.at[p])

    for p in range(NEAR, SEGMENT):
        copy(p).start()
    wide[...] = arrived_ref[...].astype(F32)
    slot = lax.broadcasted_iota(jnp.int32, (SLOTS, PEERS), 0)
    index = columns(jnp.where(slot < counts_ref[...], cells_ref[...].reshape(SLOTS, PEERS), -1))
    hots = one_hot(index, 0), one_hot(index, 1)
    found = unpack(lambda r: wide[pl.ds(r, PEERS, stride=ROWS), :], hots, 1)
    for p in range(SEGMENT):
        lines[p] = found[:, p * LINES : (p + 1) * LINES]
    row = sublane_ids()
    on_left = left(HALF)

    def force(p, blocks_ref):
        forcing = matvec(blocks_ref, p, lines[p], row)
        low, high = blocks8(forcing, 0), swap(blocks8(forcing, 1))
        forcing_a[p] = jnp.where(on_left, low, high)
        forcing_b[p] = jnp.where(on_left, high, low)

    @pl.loop(0, NEAR)
    def _(p):
        bundle_copy(p + 1).start()
        force(p, near_ref)

    @pl.loop(NEAR, SEGMENT)
    def _(p):
        copy(p).wait()

        @pl.when(p + 1 < SEGMENT)
        def _():
            bundle_copy(p + 1).start()

        force(p, inverses_ref)

    end_ref[...] = advance(
        bundle_ref, forcing_a, lambda p: bundle_copy(p).wait(), forcing_a[0]
    )


def hots_kernel(cells_ref, counts_ref, even_ref, odd_ref):
    slot = lax.broadcasted_iota(jnp.int32, (SLOTS, PEERS), 0)
    index = columns(jnp.where(slot < counts_ref[...], cells_ref[...].reshape(SLOTS, PEERS), -1))
    even_ref[...] = one_hot(index, 0)
    odd_ref[...] = one_hot(index, 1)


def here(hop):
    return lax.axis_index("circ") == hop % N_CIRC


def first_hop_kernel(
    bundle_a_hbm, bundle_b_hbm, forcing_ref, end_ref, head_ref, bundle_ref, sems, head_sem
):
    def copy(p):
        return pltpu.make_async_copy(bundle_b_hbm.at[p], bundle_ref.at[p], sems.at[p])

    for p in (*range(1, SEGMENT), 0):
        copy(p).start()
    head = pltpu.make_async_copy(bundle_a_hbm.at[pl.ds(0, 1)], head_ref, head_sem)
    head.start()
    end_ref[...] = advance(bundle_ref, forcing_ref, lambda p: copy(p).wait(), forcing_ref[0])
    copy(0).wait()
    head.wait()


def widen_kernel(after_ref, *refs):
    *heads, bundle_ref, wide_ref = refs

    def widen(p, from_ref, at):
        @pl.loop(0, HALF, unroll=8)
        def _(i):
            wide_ref[p, i] = from_ref[at, i].astype(F32)

    if heads:
        widen(0, heads[0], 0)

    @pl.loop(len(heads), SEGMENT)
    def _(p):
        widen(p, bundle_ref, p)


def second_hop_kernel(state_ref, head_ref, coupling_ref, forcing_ref, end_ref):
    @pl.when(here(1))
    def _():
        state = move(head_ref, 0, forcing_ref[0], state_ref[...])
        end_ref[...] = advance(coupling_ref, forcing_ref, 1, state)


def hop_kernel(hop, state_ref, coupling_ref, forcing_ref, end_ref):
    @pl.when(here(hop))
    def _():
        end_ref[...] = advance(coupling_ref, forcing_ref, 0, state_ref[...])


def final_kernel(*refs):
    *state_refs, coupling_ref, forcing_ref, solved_ref = refs
    state = state_refs[0][...]
    for ref in state_refs[1:]:
        state = state + ref[...]
    advance(coupling_ref, forcing_ref, 0, state, solved_ref)


def half_power(exponent):
    return jnp.exp2(0.5 * exponent)


def return_pack_kernel(solved_a, solved_b, even_ref, odd_ref, out_ref, wide):
    def store(r, block):
        wide[pl.ds(r, PEERS, stride=ROWS), :] = block

    on_left = left(HALF)
    cells = []
    for position in range(SEGMENT):
        a, b = solved_a[position], solved_b[position]
        low = jnp.where(on_left, a, b)
        high = swap(jnp.where(on_left, b, a))
        blocks = [x[j : j + 8] for j in range(0, HALF, 8) for x in (low, high)]
        cells.append(jnp.concatenate(blocks, axis=0))
    rest = jnp.concatenate(cells, axis=1)
    largest = jnp.max(jnp.abs(rest), axis=0, keepdims=True)
    exponent = jnp.ceil(jnp.log2(jnp.maximum(largest, SMALLEST)))
    shrink = half_power(-exponent)
    whole = jnp.floor(rest * shrink * shrink * STEPS + 0.5)
    high = whole.astype(BF16)
    low = (whole - high.astype(F32)).astype(BF16)
    pack([high, low], (even_ref[...], odd_ref[...]), store, exponent)
    out_ref[...] = wide[...].astype(jnp.int32).astype(jnp.int16)


def return_kernel(arrived_ref, send_ref, out_ref, wide):
    wide[...] = arrived_ref[...].astype(jnp.int32).astype(F32)
    index = columns(send_ref[...].reshape(SLOTS, PEERS))
    whole, exponent = unpack(
        lambda r: wide[pl.ds(r, PEERS, stride=ROWS), :],
        (one_hot(index, 0), one_hot(index, 1)),
        2,
        True,
    )
    grow = half_power(exponent[:1])
    out_ref[...] = whole * (1.0 / STEPS) * grow * grow


def vmem(x):
    return pltpu.with_memory_space_constraint(x, pltpu.VMEM)


def hbm(x):
    return pltpu.with_memory_space_constraint(x, pltpu.HBM)


def exchange(rows):
    blocks = rows.reshape(PEERS, ROWS, 128)
    moved = lax.all_to_all(blocks, ("circ", "span"), split_axis=0, concat_axis=0, tiled=True)
    return moved.reshape(PEERS * ROWS, 128)


def local(elem_rows, coupling, inverses, send_rows, recv_cells, slot_counts):
    send = jnp.transpose(send_rows, (2, 0, 1))
    cells = jnp.transpose(recv_cells, (2, 0, 1))
    packed_rows = (PEERS * ROWS, LANES)
    hot_shape = jax.ShapeDtypeStruct((PAIRS * PEERS, CELLS), BF16)
    bundle_shape = jax.ShapeDtypeStruct((SEGMENT, HALF, FEATURES, LANES), BF16)
    state_shape = jax.ShapeDtypeStruct((HALF, LANES), F32)
    forcing_shape = jax.ShapeDtypeStruct((SEGMENT, HALF, LANES), F32)
    in_hbm = pl.BlockSpec(memory_space=pltpu.HBM)
    outgoing = pl.pallas_call(
        pack_rows_kernel,
        out_shape=jax.ShapeDtypeStruct(packed_rows, BF16),
        in_specs=[in_hbm, IN_VMEM],
        out_specs=IN_VMEM,
        scratch_shapes=[
            pltpu.VMEM(packed_rows, F32),
            pltpu.VMEM(elem_rows.shape, BF16),
            pltpu.SemaphoreType.DMA,
        ],
        compiler_params=params(16),
        name="pack_rows",
    )(hbm(elem_rows), send)
    arrived = exchange(outgoing)
    *bundles, near = pl.pallas_call(
        bundle_kernel,
        out_shape=[pltpu.HBM(bundle_shape.shape, BF16)] * 2
        + [jax.ShapeDtypeStruct((NEAR, *inverses.shape[1:]), BF16)],
        in_specs=[in_hbm] * 2,
        out_specs=[in_hbm] * 2 + [IN_VMEM],
        scratch_shapes=[
            pltpu.VMEM(coupling.shape, BF16),
            pltpu.VMEM(bundle_shape.shape, BF16),
            pltpu.VMEM(bundle_shape.shape, BF16),
            pltpu.SemaphoreType.DMA((3, SEGMENT)),
            pltpu.SemaphoreType.DMA,
        ],
        compiler_params=params(32),
        cost_estimate=pl.CostEstimate(flops=0, bytes_accessed=4 * coupling.size, transcendentals=0),
        name="bundle",
    )(hbm(coupling), hbm(inverses))
    *forcings, bundle_a, end_a = pl.pallas_call(
        forcing_kernel,
        out_shape=[forcing_shape] * 2 + [bundle_shape, state_shape],
        in_specs=[IN_VMEM] * 4 + [in_hbm] * 2,
        out_specs=[IN_VMEM] * 4,
        scratch_shapes=[
            pltpu.VMEM(packed_rows, F32),
            pltpu.VMEM((SEGMENT, FEATURES, LINES), F32),
            pltpu.VMEM(inverses.shape, BF16),
            pltpu.SemaphoreType.DMA((SEGMENT,)),
            pltpu.SemaphoreType.DMA((SEGMENT,)),
        ],
        compiler_params=params(24),
        name="forcing",
    )(arrived, cells, slot_counts, vmem(near), hbm(inverses), hbm(bundles[0]))
    forcings = [vmem(forcing) for forcing in forcings]
    end_b, head_a, bundle_b = pl.pallas_call(
        first_hop_kernel,
        out_shape=[
            state_shape,
            jax.ShapeDtypeStruct((1, *bundle_shape.shape[1:]), BF16),
            bundle_shape,
        ],
        in_specs=[in_hbm, in_hbm, IN_VMEM],
        out_specs=[IN_VMEM] * 3,
        scratch_shapes=[pltpu.SemaphoreType.DMA((SEGMENT,)), pltpu.SemaphoreType.DMA],
        compiler_params=params(8),
        name="first_hop",
    )(hbm(bundles[0]), hbm(bundles[1]), forcings[1])
    narrow = [[vmem(head_a), vmem(bundle_a)], [vmem(bundle_b)]]
    sweep_cost = pl.CostEstimate(
        flops=2 * 10**6, bytes_accessed=2 * bundle_shape.size, transcendentals=0
    )

    def sweep(kernel, states, blocks, forcing, shape, name):
        operands = [*states, *blocks, forcing]
        return pl.pallas_call(
            kernel,
            out_shape=shape,
            in_specs=[IN_VMEM] * len(operands),
            out_specs=IN_VMEM,
            compiler_params=params(8),
            cost_estimate=sweep_cost,
            name=name,
        )(*operands)

    def widen(after, blocks):
        return vmem(
            pl.pallas_call(
                widen_kernel,
                out_shape=jax.ShapeDtypeStruct(bundle_shape.shape, F32),
                in_specs=[IN_VMEM] * (1 + len(blocks)),
                out_specs=IN_VMEM,
                compiler_params=params(4),
                cost_estimate=sweep_cost,
                name="widen",
            )(after, *blocks)
        )

    cells, counts, _ = lax.optimization_barrier((cells, slot_counts, end_b))
    even, odd = pl.pallas_call(
        hots_kernel,
        out_shape=[hot_shape] * 2,
        in_specs=[IN_VMEM] * 2,
        out_specs=[IN_VMEM] * 2,
        compiler_params=params(8),
        name="hots",
    )(cells, counts)
    arrivals = ([], [])
    blocks = narrow
    for hop in range(2 * N_CIRC - 1):
        pair = (hop % N_CIRC, (hop + 1) % N_CIRC)
        for side in range(2):
            end = (end_a, end_b)[side]
            if hop:
                kernel = functools.partial(hop_kernel, hop)
                if hop == 1 and side == 0:
                    kernel = second_hop_kernel
                end = sweep(
                    kernel, arrivals[side][-1:], blocks[side], forcings[side], state_shape, "hop_" + "ab"[side]
                )
            arrivals[side].append(lax.ppermute(end, "circ", [pair]))
        if hop == 1:
            blocks = [[widen(end, part)] for part in narrow]
    solved = [
        sweep(
            final_kernel, arrivals[side][N_CIRC - 1 :], blocks[side], forcings[side], forcing_shape, "final_" + "ab"[side]
        )
        for side in range(2)
    ]

    returning = pl.pallas_call(
        return_pack_kernel,
        out_shape=jax.ShapeDtypeStruct(packed_rows, jnp.int16),
        in_specs=[IN_VMEM] * 4,
        out_specs=IN_VMEM,
        scratch_shapes=[pltpu.VMEM(packed_rows, F32)],
        compiler_params=params(16),
        name="return_pack",
    )(*solved, vmem(even), vmem(odd))
    returned = exchange(returning)
    return pl.pallas_call(
        return_kernel,
        out_shape=jax.ShapeDtypeStruct((FEATURES, CELLS), F32),
        in_specs=[IN_VMEM] * 2,
        out_specs=IN_VMEM,
        scratch_shapes=[pltpu.VMEM(packed_rows, F32)],
        compiler_params=params(16),
        name="return_rows",
    )(returned, send)


def solution(mesh):
    return jax.shard_map(
        local,
        mesh=mesh,
        in_specs=(
            P(None, ("circ", "span")),
            P("circ", None, None, "span"),
            P("circ", None, None, "span"),
            P(("circ", "span"), None, None),
            P(("circ", "span"), None, None),
            P(("circ", "span"), None),
        ),
        out_specs=P(None, ("circ", "span")),
        check_vma=False,
    )
```

profile of v0, /device:TPU:1, one launch (start us, length us, event | category | flops | bytes accessed | tf_op | source)
XLA Modules:
  0.0 133.8 jit_solution(16482959779005297365)
XLA Ops:
  0.0 0.7 copy-done.1
  0.7 2.5 %pack_rows.1 = bf16[1024,128]{1,0:T(8,128)(2,1)} custom-call(bf16[80,768]{1,0:T(8,128)(2,1)} %rows_hbm.1, s32[12,1,128]{2,1,0:T(1,128)S(1)} %bitcast.11), custom_call_target="tpu_custom_call" | custom-call | tf_op jit(solution)/shard_map/pack_rows/pallas_call | solution.py:417
  3.2 11.5 %all-to-all-start = ((bf16[128,8,128]{2,1,0:T(8,128)(2,1)}), bf16[128,8,128]{2,1,0:T(8,128)(2,1)S(1)}, u32[]{:S(2)}, u32[]{:S(2)}) async-start(bf16[128,8,128]{2,1,0:T(8,128)(2,1)} %bitcast.1), calls=%async_computation | async-start | bytes 524288 | tf_op jit(solution)/shard_map/all_to_all | solution.py:404
  14.7 8.4 %bundle.1 = (bf16[6,40,80,128]{3,2,1,0:T(8,128)(2,1)}, bf16[6,40,80,128]{3,2,1,0:T(8,128)(2,1)}, bf16[2,80,80,128]{3,2,1,0:T(8,128)(2,1)S(1)}) custom-call(bf16[6,80,80,128]{3,2,1,0:T(8,128)(2,1)} %coupling_hbm.1, bf16[6,80,80,128]{3,2,1,0:T(8,128)(2,1)} %inverses_hbm.3), custom_call_target="tpu_custom_call" | custom-call | bytes 19660800 | tf_op jit(solution)/shard_map/bundle/pallas_call | solution.py:431
  23.1 2.4 %all-to-all-done = bf16[128,8,128]{2,1,0:T(8,128)(2,1)S(1)} async-done(((bf16[128,8,128]{2,1,0:T(8,128)(2,1)}), bf16[128,8,128]{2,1,0:T(8,128)(2,1)S(1)}, u32[]{:S(2)}, u32[]{:S(2)}) %all-to-all-start) | async-done | bytes 262176 | tf_op jit(solution)/shard_map/all_to_all | solution.py:404
  25.6 4.6 %forcing.1 = (f32[6,40,128]{2,1,0:T(8,128)S(1)}, f32[6,40,128]{2,1,0:T(8,128)S(1)}, bf16[6,40,80,128]{3,2,1,0:T(8,128)(2,1)S(1)}, f32[40,128]{1,0:T(8,128)S(1)}) custom-call(bf16[1024,128]{1,0:T(8,128)(2,1)S(1)} %bitcast.6, s32[12,1,128]{2,1,0:T(1,128)S(1)} %bitcast.9, s32[1,128]{1,0:T(1,128)S(1)} %copy-done.3, ...), custom_call_target="tpu_custom_call" | custom-call | tf_op jit(solution)/shard_map/forcing/pallas_call | solution.py:448
  30.2 1.6 %collective-permute-start = (f32[40,128]{1,0:T(8,128)S(1)}, f32[40,128]{1,0:T(8,128)S(1)}, u32[]{:S(2)}, u32[]{:S(2)}) collective-permute-start(f32[40,128]{1,0:T(8,128)S(1)} %get-tuple-element.21), channel_id=1, source_target_pairs={{0,16},{1,17},{2,18},{3,19},{4,20},{5,21},{6,22},{7,23},{8,24},{9,... | collective-permute-start | bytes 61448 | tf_op jit(solution)/shard_map/ppermute | solution.py:529
  31.8 2.7 %first_hop.1 = (f32[40,128]{1,0:T(8,128)S(1)}, bf16[1,40,80,128]{3,2,1,0:T(8,128)(2,1)S(1)}, bf16[6,40,80,128]{3,2,1,0:T(8,128)(2,1)S(1)}) custom-call(bf16[6,40,80,128]{3,2,1,0:T(8,128)(2,1)} %get-tuple-element.20.bundle_hbm.bundle_a_hbm, bf16[6,40,80,128]{3,2,1,0:T(8,128)(2,1)} %get-tuple-element.22.bundle_b_hbm, ...), custom_call_target="tpu_custom_call" | custom-call | tf_op jit(solution)/shard_map/first_hop/pallas_call | solution.py:464
  34.5 1.3 collective-permute-start.2
  35.8 0.7 collective-permute-start.1
  36.7 0.7 collective-permute-start.16
  37.3 0.8 widen.2.coupling_ref.refs_8_
  38.2 0.8 widen.3.coupling_ref.refs_8_
  39.0 0.7 collective-permute-start.3
  39.7 0.7 collective-permute-start.17
  40.4 0.7 collective-permute-start.4
  41.1 0.7 collective-permute-start.18
  41.8 0.7 collective-permute-start.5
  42.5 0.7 collective-permute-start.19
  43.2 0.7 collective-permute-start.6
  44.0 0.7 collective-permute-start.20
  44.7 0.7 collective-permute-start.7
  45.4 0.7 collective-permute-start.21
  46.1 1.3 collective-permute-start.8
  47.4 1.3 collective-permute-start.22
  48.7 16.4 %collective-permute-done.8.state_ref.refs_0_ = f32[40,128]{1,0:T(8,128)S(1)} collective-permute-done((f32[40,128]{1,0:T(8,128)S(1)}, f32[40,128]{1,0:T(8,128)S(1)}, u32[]{:S(2)}, u32[]{:S(2)}) %collective-permute-start.8) | collective-permute-done | bytes 20512 | tf_op jit(solution)/shard_map/ppermute | solution.py:529
  65.1 0.9 hop_a.21
  66.0 1.3 collective-permute-start.9
  67.3 1.1 collective-permute-done.22.state_ref.refs_0_
  68.3 0.9 hop_b.21
  69.2 1.3 collective-permute-start.23
  70.7 0.7 collective-permute-start.10
  71.4 0.7 collective-permute-start.24
  72.1 0.7 collective-permute-start.11
  72.8 0.7 collective-permute-start.25
  73.5 0.7 collective-permute-start.12
  74.2 0.7 collective-permute-start.26
  74.9 0.7 collective-permute-start.13
  75.6 0.7 collective-permute-start.27
  76.3 0.7 collective-permute-start.14
  77.0 0.7 collective-permute-start.28
  77.8 0.7 collective-permute-start.15
  78.5 0.7 collective-permute-start.29
  79.7 0.9 final_a.1.solved_a
  80.6 0.9 final_b.1.solved_b
  81.4 1.6 %return_pack.1 = s16[1024,128]{1,0:T(8,128)(2,1)S(1)} custom-call(f32[6,40,128]{2,1,0:T(8,128)S(1)} %final_a.1.solved_a, f32[6,40,128]{2,1,0:T(8,128)S(1)} %final_b.1.solved_b, bf16[768,768]{1,0:T(8,128)(2,1)S(1)} %get-tuple-element.31.even_ref, bf16[768,768]{1,0:T(8,128)(2,1)S(1)} %get-tuple-element.32.odd_ref), custom_call_target="tpu_custom_call" | custom-call | tf_op jit(solution)/shard_map/return_pack/pallas_call | solution.py:539
  83.1 48.0 %all_to_all.10 = s16[128,8,128]{2,1,0:T(8,128)(2,1)S(1)} all-to-all(s16[128,8,128]{2,1,0:T(8,128)(2,1)S(1)} %bitcast.8), channel_id=1, replica_groups=mesh['circ'=8,'span'=16] {'circ','span'}, dimensions={0} | all-to-all | bytes 524288 | tf_op jit(solution)/shard_map/all_to_all | solution.py:404
  131.1 2.7 %return_rows.1 = f32[80,768]{1,0:T(8,128)} custom-call(s16[1024,128]{1,0:T(8,128)(2,1)S(1)} %bitcast.7, s32[12,1,128]{2,1,0:T(1,128)S(1)} %bitcast.12), custom_call_target="tpu_custom_call" | custom-call | tf_op jit(solution)/shard_map/return_rows/pallas_call | solution.py:549
  (62 shorter events, 1.4 us)
Async XLA Ops:
  0.0 0.7 copy-start.1
  3.2 22.4 %all-to-all-start = ((bf16[128,8,128]{2,1,0:T(8,128)(2,1)}), bf16[128,8,128]{2,1,0:T(8,128)(2,1)S(1)}, u32[]{:S(2)}, u32[]{:S(2)}) async-start(bf16[128,8,128]{2,1,0:T(8,128)(2,1)} %bitcast.1), calls=%async_computation | async-start | bytes 524288 | tf_op jit(solution)/shard_map/all_to_all | solution.py:404
  14.7 10.9 %copy-start = (s32[1,128,12]{1,0,2:T(1,128)S(1)}, s32[1,128,12]{1,0,2:T(1,128)}, u32[]{:S(2)}) copy-start(s32[1,128,12]{1,0,2:T(1,128)} %param.10) | copy-start | bytes 18436
  14.7 10.8 %copy-start.3 = (s32[1,128]{1,0:T(1,128)S(1)}, s32[1,128]{1,0:T(1,128)}, u32[]{:S(2)}) copy-start(s32[1,128]{1,0:T(1,128)} %counts_ref.2) | copy-start | bytes 1540
  30.2 5.6 %collective-permute-start = (f32[40,128]{1,0:T(8,128)S(1)}, f32[40,128]{1,0:T(8,128)S(1)}, u32[]{:S(2)}, u32[]{:S(2)}) collective-permute-start(f32[40,128]{1,0:T(8,128)S(1)} %get-tuple-element.21), channel_id=1, source_target_pairs={{0,16},{1,17},{2,18},{3,19},{4,20},{5,21},{6,22},{7,23},{8,24},{9,... | collective-permute-start | bytes 61448 | tf_op jit(solution)/shard_map/ppermute | solution.py:529
  34.5 2.2 %collective-permute-start.2 = (f32[40,128]{1,0:T(8,128)S(1)}, f32[40,128]{1,0:T(8,128)S(1)}, u32[]{:S(2)}, u32[]{:S(2)}) collective-permute-start(f32[40,128]{1,0:T(8,128)S(1)} %get-tuple-element.27), channel_id=1, source_target_pairs={{0,16},{1,17},{2,18},{3,19},{4,20},{5,21},{6,22},{7,23},{8,24},{9,... | collective-permute-start | bytes 61448 | tf_op jit(solution)/shard_map/ppermute | solution.py:529
  35.8 3.2 %collective-permute-start.1 = (f32[40,128]{1,0:T(8,128)S(1)}, f32[40,128]{1,0:T(8,128)S(1)}, u32[]{:S(2)}, u32[]{:S(2)}) collective-permute-start(f32[40,128]{1,0:T(8,128)S(1)} %hop_a.14), channel_id=1, source_target_pairs={{16,32},{17,33},{18,34},{19,35},{20,36},{21,37},{22,38},{23,39},{2... | collective-permute-start | bytes 61448 | tf_op jit(solution)/shard_map/ppermute | solution.py:529
  36.7 3.0 %collective-permute-start.16 = (f32[40,128]{1,0:T(8,128)S(1)}, f32[40,128]{1,0:T(8,128)S(1)}, u32[]{:S(2)}, u32[]{:S(2)}) collective-permute-start(f32[40,128]{1,0:T(8,128)S(1)} %hop_b.14.after_ref), channel_id=1, source_target_pairs={{16,32},{17,33},{18,34},{19,35},{20,36},{21,37},{22,38},{23,39},{2... | collective-permute-start | bytes 61448 | tf_op jit(solution)/shard_map/ppermute | solution.py:529
  39.0 1.4 %collective-permute-start.3 = (f32[40,128]{1,0:T(8,128)S(1)}, f32[40,128]{1,0:T(8,128)S(1)}, u32[]{:S(2)}, u32[]{:S(2)}) collective-permute-start(f32[40,128]{1,0:T(8,128)S(1)} %hop_a.15), channel_id=1, source_target_pairs={{32,48},{33,49},{34,50},{35,51},{36,52},{37,53},{38,54},{39,55},{4... | collective-permute-start | bytes 61448 | tf_op jit(solution)/shard_map/ppermute | solution.py:529
  39.7 1.4 %collective-permute-start.17 = (f32[40,128]{1,0:T(8,128)S(1)}, f32[40,128]{1,0:T(8,128)S(1)}, u32[]{:S(2)}, u32[]{:S(2)}) collective-permute-start(f32[40,128]{1,0:T(8,128)S(1)} %hop_b.15), channel_id=1, source_target_pairs={{32,48},{33,49},{34,50},{35,51},{36,52},{37,53},{38,54},{39,55},{4... | collective-permute-start | bytes 61448 | tf_op jit(solution)/shard_map/ppermute | solution.py:529
  40.4 1.4 %collective-permute-start.4 = (f32[40,128]{1,0:T(8,128)S(1)}, f32[40,128]{1,0:T(8,128)S(1)}, u32[]{:S(2)}, u32[]{:S(2)}) collective-permute-start(f32[40,128]{1,0:T(8,128)S(1)} %hop_a.16), channel_id=1, source_target_pairs={{48,64},{49,65},{50,66},{51,67},{52,68},{53,69},{54,70},{55,71},{5... | collective-permute-start | bytes 61448 | tf_op jit(solution)/shard_map/ppermute | solution.py:529
  41.1 1.4 %collective-permute-start.18 = (f32[40,128]{1,0:T(8,128)S(1)}, f32[40,128]{1,0:T(8,128)S(1)}, u32[]{:S(2)}, u32[]{:S(2)}) collective-permute-start(f32[40,128]{1,0:T(8,128)S(1)} %hop_b.16), channel_id=1, source_target_pairs={{48,64},{49,65},{50,66},{51,67},{52,68},{53,69},{54,70},{55,71},{5... | collective-permute-start | bytes 61448 | tf_op jit(solution)/shard_map/ppermute | solution.py:529
  41.8 1.4 %collective-permute-start.5 = (f32[40,128]{1,0:T(8,128)S(1)}, f32[40,128]{1,0:T(8,128)S(1)}, u32[]{:S(2)}, u32[]{:S(2)}) collective-permute-start(f32[40,128]{1,0:T(8,128)S(1)} %hop_a.17), channel_id=1, source_target_pairs={{64,80},{65,81},{66,82},{67,83},{68,84},{69,85},{70,86},{71,87},{7... | collective-permute-start | bytes 61448 | tf_op jit(solution)/shard_map/ppermute | solution.py:529
  42.5 1.4 %collective-permute-start.19 = (f32[40,128]{1,0:T(8,128)S(1)}, f32[40,128]{1,0:T(8,128)S(1)}, u32[]{:S(2)}, u32[]{:S(2)}) collective-permute-start(f32[40,128]{1,0:T(8,128)S(1)} %hop_b.17), channel_id=1, source_target_pairs={{64,80},{65,81},{66,82},{67,83},{68,84},{69,85},{70,86},{71,87},{7... | collective-permute-start | bytes 61448 | tf_op jit(solution)/shard_map/ppermute | solution.py:529
  43.2 1.4 %collective-permute-start.6 = (f32[40,128]{1,0:T(8,128)S(1)}, f32[40,128]{1,0:T(8,128)S(1)}, u32[]{:S(2)}, u32[]{:S(2)}) collective-permute-start(f32[40,128]{1,0:T(8,128)S(1)} %hop_a.18), channel_id=1, source_target_pairs={{80,96},{81,97},{82,98},{83,99},{84,100},{85,101},{86,102},{87,103... | collective-permute-start | bytes 61448 | tf_op jit(solution)/shard_map/ppermute | solution.py:529
  44.0 1.4 %collective-permute-start.20 = (f32[40,128]{1,0:T(8,128)S(1)}, f32[40,128]{1,0:T(8,128)S(1)}, u32[]{:S(2)}, u32[]{:S(2)}) collective-permute-start(f32[40,128]{1,0:T(8,128)S(1)} %hop_b.18), channel_id=1, source_target_pairs={{80,96},{81,97},{82,98},{83,99},{84,100},{85,101},{86,102},{87,103... | collective-permute-start | bytes 61448 | tf_op jit(solution)/shard_map/ppermute | solution.py:529
  44.7 1.4 %collective-permute-start.7 = (f32[40,128]{1,0:T(8,128)S(1)}, f32[40,128]{1,0:T(8,128)S(1)}, u32[]{:S(2)}, u32[]{:S(2)}) collective-permute-start(f32[40,128]{1,0:T(8,128)S(1)} %hop_a.19), channel_id=1, source_target_pairs={{96,112},{97,113},{98,114},{99,115},{100,116},{101,117},{102,118},... | collective-permute-start | bytes 61448 | tf_op jit(solution)/shard_map/ppermute | solution.py:529
  45.4 2.0 %collective-permute-start.21 = (f32[40,128]{1,0:T(8,128)S(1)}, f32[40,128]{1,0:T(8,128)S(1)}, u32[]{:S(2)}, u32[]{:S(2)}) collective-permute-start(f32[40,128]{1,0:T(8,128)S(1)} %hop_b.19), channel_id=1, source_target_pairs={{96,112},{97,113},{98,114},{99,115},{100,116},{101,117},{102,118},... | collective-permute-start | bytes 61448 | tf_op jit(solution)/shard_map/ppermute | solution.py:529
  46.1 19.0 %collective-permute-start.8 = (f32[40,128]{1,0:T(8,128)S(1)}, f32[40,128]{1,0:T(8,128)S(1)}, u32[]{:S(2)}, u32[]{:S(2)}) collective-permute-start(f32[40,128]{1,0:T(8,128)S(1)} %hop_a.20), channel_id=1, source_target_pairs={{112,0},{113,1},{114,2},{115,3},{116,4},{117,5},{118,6},{119,7},{1... | collective-permute-start | bytes 61448 | tf_op jit(solution)/shard_map/ppermute | solution.py:529
  47.4 20.9 %collective-permute-start.22 = (f32[40,128]{1,0:T(8,128)S(1)}, f32[40,128]{1,0:T(8,128)S(1)}, u32[]{:S(2)}, u32[]{:S(2)}) collective-permute-start(f32[40,128]{1,0:T(8,128)S(1)} %hop_b.20), channel_id=1, source_target_pairs={{112,0},{113,1},{114,2},{115,3},{116,4},{117,5},{118,6},{119,7},{1... | collective-permute-start | bytes 61448 | tf_op jit(solution)/shard_map/ppermute | solution.py:529
  66.0 4.5 %collective-permute-start.9 = (f32[40,128]{1,0:T(8,128)S(1)}, f32[40,128]{1,0:T(8,128)S(1)}, u32[]{:S(2)}, u32[]{:S(2)}) collective-permute-start(f32[40,128]{1,0:T(8,128)S(1)} %hop_a.21), channel_id=1, source_target_pairs={{0,16},{1,17},{2,18},{3,19},{4,20},{5,21},{6,22},{7,23},{8,24},{9,... | collective-permute-start | bytes 61448 | tf_op jit(solution)/shard_map/ppermute | solution.py:529
  69.2 2.2 %collective-permute-start.23 = (f32[40,128]{1,0:T(8,128)S(1)}, f32[40,128]{1,0:T(8,128)S(1)}, u32[]{:S(2)}, u32[]{:S(2)}) collective-permute-start(f32[40,128]{1,0:T(8,128)S(1)} %hop_b.21), channel_id=1, source_target_pairs={{0,16},{1,17},{2,18},{3,19},{4,20},{5,21},{6,22},{7,23},{8,24},{9,... | collective-permute-start | bytes 61448 | tf_op jit(solution)/shard_map/ppermute | solution.py:529
  70.7 1.4 %collective-permute-start.10 = (f32[40,128]{1,0:T(8,128)S(1)}, f32[40,128]{1,0:T(8,128)S(1)}, u32[]{:S(2)}, u32[]{:S(2)}) collective-permute-start(f32[40,128]{1,0:T(8,128)S(1)} %hop_a.22), channel_id=1, source_target_pairs={{16,32},{17,33},{18,34},{19,35},{20,36},{21,37},{22,38},{23,39},{2... | collective-permute-start | bytes 61448 | tf_op jit(solution)/shard_map/ppermute | solution.py:529
  71.4 1.4 %collective-permute-start.24 = (f32[40,128]{1,0:T(8,128)S(1)}, f32[40,128]{1,0:T(8,128)S(1)}, u32[]{:S(2)}, u32[]{:S(2)}) collective-permute-start(f32[40,128]{1,0:T(8,128)S(1)} %hop_b.22), channel_id=1, source_target_pairs={{16,32},{17,33},{18,34},{19,35},{20,36},{21,37},{22,38},{23,39},{2... | collective-permute-start | bytes 61448 | tf_op jit(solution)/shard_map/ppermute | solution.py:529
  72.1 1.4 %collective-permute-start.11 = (f32[40,128]{1,0:T(8,128)S(1)}, f32[40,128]{1,0:T(8,128)S(1)}, u32[]{:S(2)}, u32[]{:S(2)}) collective-permute-start(f32[40,128]{1,0:T(8,128)S(1)} %hop_a.23), channel_id=1, source_target_pairs={{32,48},{33,49},{34,50},{35,51},{36,52},{37,53},{38,54},{39,55},{4... | collective-permute-start | bytes 61448 | tf_op jit(solution)/shard_map/ppermute | solution.py:529
  72.8 1.4 %collective-permute-start.25 = (f32[40,128]{1,0:T(8,128)S(1)}, f32[40,128]{1,0:T(8,128)S(1)}, u32[]{:S(2)}, u32[]{:S(2)}) collective-permute-start(f32[40,128]{1,0:T(8,128)S(1)} %hop_b.23), channel_id=1, source_target_pairs={{32,48},{33,49},{34,50},{35,51},{36,52},{37,53},{38,54},{39,55},{4... | collective-permute-start | bytes 61448 | tf_op jit(solution)/shard_map/ppermute | solution.py:529
  73.5 1.4 %collective-permute-start.12 = (f32[40,128]{1,0:T(8,128)S(1)}, f32[40,128]{1,0:T(8,128)S(1)}, u32[]{:S(2)}, u32[]{:S(2)}) collective-permute-start(f32[40,128]{1,0:T(8,128)S(1)} %hop_a.24), channel_id=1, source_target_pairs={{48,64},{49,65},{50,66},{51,67},{52,68},{53,69},{54,70},{55,71},{5... | collective-permute-start | bytes 61448 | tf_op jit(solution)/shard_map/ppermute | solution.py:529
  74.2 1.4 %collective-permute-start.26 = (f32[40,128]{1,0:T(8,128)S(1)}, f32[40,128]{1,0:T(8,128)S(1)}, u32[]{:S(2)}, u32[]{:S(2)}) collective-permute-start(f32[40,128]{1,0:T(8,128)S(1)} %hop_b.24), channel_id=1, source_target_pairs={{48,64},{49,65},{50,66},{51,67},{52,68},{53,69},{54,70},{55,71},{5... | collective-permute-start | bytes 61448 | tf_op jit(solution)/shard_map/ppermute | solution.py:529
  74.9 1.4 %collective-permute-start.13 = (f32[40,128]{1,0:T(8,128)S(1)}, f32[40,128]{1,0:T(8,128)S(1)}, u32[]{:S(2)}, u32[]{:S(2)}) collective-permute-start(f32[40,128]{1,0:T(8,128)S(1)} %hop_a.25), channel_id=1, source_target_pairs={{64,80},{65,81},{66,82},{67,83},{68,84},{69,85},{70,86},{71,87},{7... | collective-permute-start | bytes 61448 | tf_op jit(solution)/shard_map/ppermute | solution.py:529
  75.6 1.4 %collective-permute-start.27 = (f32[40,128]{1,0:T(8,128)S(1)}, f32[40,128]{1,0:T(8,128)S(1)}, u32[]{:S(2)}, u32[]{:S(2)}) collective-permute-start(f32[40,128]{1,0:T(8,128)S(1)} %hop_b.25), channel_id=1, source_target_pairs={{64,80},{65,81},{66,82},{67,83},{68,84},{69,85},{70,86},{71,87},{7... | collective-permute-start | bytes 61448 | tf_op jit(solution)/shard_map/ppermute | solution.py:529
  76.3 1.4 %collective-permute-start.14 = (f32[40,128]{1,0:T(8,128)S(1)}, f32[40,128]{1,0:T(8,128)S(1)}, u32[]{:S(2)}, u32[]{:S(2)}) collective-permute-start(f32[40,128]{1,0:T(8,128)S(1)} %hop_a.26), channel_id=1, source_target_pairs={{80,96},{81,97},{82,98},{83,99},{84,100},{85,101},{86,102},{87,103... | collective-permute-start | bytes 61448 | tf_op jit(solution)/shard_map/ppermute | solution.py:529
  77.0 1.4 %collective-permute-start.28 = (f32[40,128]{1,0:T(8,128)S(1)}, f32[40,128]{1,0:T(8,128)S(1)}, u32[]{:S(2)}, u32[]{:S(2)}) collective-permute-start(f32[40,128]{1,0:T(8,128)S(1)} %hop_b.26), channel_id=1, source_target_pairs={{80,96},{81,97},{82,98},{83,99},{84,100},{85,101},{86,102},{87,103... | collective-permute-start | bytes 61448 | tf_op jit(solution)/shard_map/ppermute | solution.py:529
  77.8 1.9 %collective-permute-start.15 = (f32[40,128]{1,0:T(8,128)S(1)}, f32[40,128]{1,0:T(8,128)S(1)}, u32[]{:S(2)}, u32[]{:S(2)}) collective-permute-start(f32[40,128]{1,0:T(8,128)S(1)} %hop_a.27), channel_id=1, source_target_pairs={{96,112},{97,113},{98,114},{99,115},{100,116},{101,117},{102,118},... | collective-permute-start | bytes 61448 | tf_op jit(solution)/shard_map/ppermute | solution.py:529
  78.5 2.1 %collective-permute-start.29 = (f32[40,128]{1,0:T(8,128)S(1)}, f32[40,128]{1,0:T(8,128)S(1)}, u32[]{:S(2)}, u32[]{:S(2)}) collective-permute-start(f32[40,128]{1,0:T(8,128)S(1)} %hop_b.27), channel_id=1, source_target_pairs={{96,112},{97,113},{98,114},{99,115},{100,116},{101,117},{102,118},... | collective-permute-start | bytes 61448 | tf_op jit(solution)/shard_map/ppermute | solution.py:529
  80.5 50.6 %copy-start.2 = (s32[1,128,12]{1,0,2:T(1,128)S(1)}, s32[1,128,12]{1,0,2:T(1,128)}, u32[]{:S(2)}) copy-start(s32[1,128,12]{1,0,2:T(1,128)} %param.9) | copy-start | bytes 18436
where the time goes:
time: 134 us
  blocking collectives  48 us (36%)
  starting transfers between devices  35.5 us (26%)
  Pallas kernels  28.6 us (21%)
  waiting for transfers between devices  20.2 us (15%)
    all_to_all x1, blocking collectives, exchange(): lax.all_to_all(blocks, ('circ', 'span'), split_axis=0, concat_axis=0, til...  48 us
    ppermute x30, starting transfers between devices, local(): arrivals[side].append(lax.ppermute(end, 'circ', [pair]))  24 us
    ppermute x30, waiting for transfers between devices, local(): arrivals[side].append(lax.ppermute(end, 'circ', [pair]))  17.7 us
    all_to_all x1, starting transfers between devices, exchange(): lax.all_to_all(blocks, ('circ', 'span'), split_axis=0, concat_axis=0, til...  11.5 us
    pallas_call x1, Pallas kernels, local(): pl.pallas_call(bundle_kernel, out_shape=[pltpu.HBM(bundle_shape.shape, BF...  8.38 us
    pallas_call x1, Pallas kernels, local(): pl.pallas_call(forcing_kernel, out_shape=[forcing_shape] * 2 + [bundle_sh...  4.58 us
    pallas_call x30, Pallas kernels, sweep(): pl.pallas_call(kernel, out_shape=shape, in_specs=[IN_VMEM] * len(operands...  4.05 us
    pallas_call x1, Pallas kernels, local(): pl.pallas_call(first_hop_kernel, out_shape=[state_shape, jax.ShapeDtypeSt...  2.69 us
  transfers between devices with their start and end apart: 31, of which 4 were waited for; matrix products, arithmetic and copies ran while one was open for 0% of the time, Pallas kernels for 12%

commit v1 on v0

--- a/solution.py
+++ b/solution.py
@@ -178,6 +178,22 @@
     out_ref[...] = wide[...].astype(BF16)
 
 
+def bundle_rows(whole, bundle_a, bundle_b, p):
+    on_left = left(FEATURES)
+
+    @pl.loop(0, HALF // 8)
+    def _(block):
+        for k in range(8):
+            low = whole[p, block * 16 + k]
+            high = whole[p, block * 16 + 8 + k].astype(F32)
+            high = jnp.concatenate(
+                [swap(high[j * 8 : j * 8 + 8]) for i in range(HALF // 8) for j in (2 * i + 1, 2 * i)],
+                axis=0,
+            ).astype(BF16)
+            bundle_a[p, block * 8 + k] = jnp.where(on_left, low, high)
+            bundle_b[p, block * 8 + k] = jnp.where(on_left, high, low)
+
+
 def bundle_kernel(
     coupling_hbm, inverses_hbm, bundle_a_hbm, bundle_b_hbm, near_ref,
     whole, bundle_a, bundle_b, sems, near_sem,
@@ -188,29 +204,16 @@
             ((coupling_hbm, whole), (bundle_a, bundle_a_hbm), (bundle_b, bundle_b_hbm))
         )
     ]
-    for copy in fetch:
+    for copy in fetch[1:]:
         copy.start()
     near = pltpu.make_async_copy(inverses_hbm.at[pl.ds(0, NEAR)], near_ref, near_sem)
     near.start()
-    on_left = left(FEATURES)
-    for p in range(SEGMENT):
+    for p in range(1, SEGMENT):
         fetch[p].wait()
-
-        @pl.loop(0, HALF // 8)
-        def _(block):
-            for k in range(8):
-                low = whole[p, block * 16 + k]
-                high = whole[p, block * 16 + 8 + k].astype(F32)
-                high = jnp.concatenate(
-                    [swap(high[j * 8 : j * 8 + 8]) for i in range(HALF // 8) for j in (2 * i + 1, 2 * i)],
-                    axis=0,
-                ).astype(BF16)
-                bundle_a[p, block * 8 + k] = jnp.where(on_left, low, high)
-                bundle_b[p, block * 8 + k] = jnp.where(on_left, high, low)
-
+        bundle_rows(whole, bundle_a, bundle_b, p)
         put_a[p].start()
         put_b[p].start()
-    for copy in put_a + put_b:
+    for copy in put_a[1:] + put_b[1:]:
         copy.wait()
     near.wait()
 
@@ -299,19 +302,20 @@
     return lax.axis_index("circ") == hop % N_CIRC
 
 
-def first_hop_kernel(
-    bundle_a_hbm, bundle_b_hbm, forcing_ref, end_ref, head_ref, bundle_ref, sems, head_sem
-):
+def first_hop_kernel(bundle_hbm, forcing_ref, end_ref, bundle_ref, sems):
     def copy(p):
-        return pltpu.make_async_copy(bundle_b_hbm.at[p], bundle_ref.at[p], sems.at[p])
-
-    for p in (*range(1, SEGMENT), 0):
+        return pltpu.make_async_copy(bundle_hbm.at[p], bundle_ref.at[p], sems.at[p])
+
+    for p in range(1, SEGMENT):
         copy(p).start()
-    head = pltpu.make_async_copy(bundle_a_hbm.at[pl.ds(0, 1)], head_ref, head_sem)
+    end_ref[...] = advance(bundle_ref, forcing_ref, lambda p: copy(p).wait(), forcing_ref[0])
+
+
+def heads_kernel(after_ref, coupling_hbm, head_a, head_b, whole, sem):
+    head = pltpu.make_async_copy(coupling_hbm.at[pl.ds(0, 1)], whole, sem)
     head.start()
-    end_ref[...] = advance(bundle_ref, forcing_ref, lambda p: copy(p).wait(), forcing_ref[0])
-    copy(0).wait()
     head.wait()
+    bundle_rows(whole, head_a, head_b, 0)
 
 
 def widen_kernel(after_ref, *refs):
@@ -461,20 +465,30 @@
         name="forcing",
     )(arrived, cells, slot_counts, vmem(near), hbm(inverses), hbm(bundles[0]))
     forcings = [vmem(forcing) for forcing in forcings]
-    end_b, head_a, bundle_b = pl.pallas_call(
+    head_shape = jax.ShapeDtypeStruct((1, *bundle_shape.shape[1:]), BF16)
+    end_b, bundle_b = pl.pallas_call(
         first_hop_kernel,
-        out_shape=[
-            state_shape,
-            jax.ShapeDtypeStruct((1, *bundle_shape.shape[1:]), BF16),
-            bundle_shape,
-        ],
-        in_specs=[in_hbm, in_hbm, IN_VMEM],
-        out_specs=[IN_VMEM] * 3,
-        scratch_shapes=[pltpu.SemaphoreType.DMA((SEGMENT,)), pltpu.SemaphoreType.DMA],
+        out_shape=[state_shape, bundle_shape],
+        in_specs=[in_hbm, IN_VMEM],
+        out_specs=[IN_VMEM] * 2,
+        scratch_shapes=[pltpu.SemaphoreType.DMA((SEGMENT,))],
         compiler_params=params(8),
         name="first_hop",
-    )(hbm(bundles[0]), hbm(bundles[1]), forcings[1])
-    narrow = [[vmem(head_a), vmem(bundle_a)], [vmem(bundle_b)]]
+    )(hbm(bundles[1]), forcings[1])
+    head_a, head_b = pl.pallas_call(
+        heads_kernel,
+        out_shape=[head_shape, head_shape],
+        in_specs=[IN_VMEM, in_hbm],
+        out_specs=[IN_VMEM] * 2,
+        scratch_shapes=[
+            pltpu.VMEM((1, *coupling.shape[1:]), BF16),
+            pltpu.SemaphoreType.DMA,
+        ],
+        compiler_params=params(8),
+        cost_estimate=pl.CostEstimate(flops=10**6, bytes_accessed=4 * 10**6, transcendentals=0),
+        name="heads",
+    )(end_b, hbm(coupling))
+    narrow = [[vmem(head_a), vmem(bundle_a)], [vmem(head_b), vmem(bundle_b)]]
     sweep_cost = pl.CostEstimate(
         flops=2 * 10**6, bytes_accessed=2 * bundle_shape.size, transcendentals=0
     )
@@ -521,7 +535,7 @@
             end = (end_a, end_b)[side]
             if hop:
                 kernel = functools.partial(hop_kernel, hop)
-                if hop == 1 and side == 0:
+                if hop == 1:
                     kernel = second_hop_kernel
                 end = sweep(
                     kernel, arrivals[side][-1:], blocks[side], forcings[side], state_shape, "hop_" + "ab"[side]

time: 134 us -> 133 us (level)
  blocking collectives: 48 us -> 45.6 us
    all_to_all x1, blocking collectives: 48 us -> 45.6 us  [exchange(): lax.all_to_all(blocks, ('circ', 'span'), split_axis=0, concat_axis=0, til...]
    pallas_call x1 -> x2, Pallas kernels: 2.69 us -> 4.49 us  [the longest x1 2.39 us: local(): pl.pallas_call(first_hop_kernel, out_shape=[state_shape, bundle_shape], i...]
  transfers between devices with their start and end apart: 31 -> 31, of which waited for: 4 -> 4; matrix products, arithmetic and copies ran while one was open for 0% -> 0% of each run, Pallas kernels for 12% -> 13%
where the time goes in v1:
time: 133 us
  blocking collectives  45.6 us (34%)
  starting transfers between devices  35.5 us (27%)
  Pallas kernels  29.3 us (22%)
  waiting for transfers between devices  20.8 us (16%)
    all_to_all x1, blocking collectives, exchange(): lax.all_to_all(blocks, ('circ', 'span'), split_axis=0, concat_axis=0, til...  45.6 us
    ppermute x30, starting transfers between devices, local(): arrivals[side].append(lax.ppermute(end, 'circ', [pair]))  24 us
    ppermute x30, waiting for transfers between devices, local(): arrivals[side].append(lax.ppermute(end, 'circ', [pair]))  17.4 us
    all_to_all x1, starting transfers between devices, exchange(): lax.all_to_all(blocks, ('circ', 'span'), split_axis=0, concat_axis=0, til...  11.5 us
    pallas_call x1, Pallas kernels, local(): pl.pallas_call(bundle_kernel, out_shape=[pltpu.HBM(bundle_shape.shape, BF...  7.39 us
    pallas_call x1, Pallas kernels, local(): pl.pallas_call(forcing_kernel, out_shape=[forcing_shape] * 2 + [bundle_sh...  4.59 us
    pallas_call x30, Pallas kernels, sweep(): pl.pallas_call(kernel, out_shape=shape, in_specs=[IN_VMEM] * len(operands...  3.87 us
    all_to_all x1, waiting for transfers between devices, exchange(): lax.all_to_all(blocks, ('circ', 'span'), split_axis=0, concat_axis=0, til...  3.4 us
  transfers between devices with their start and end apart: 31, of which 4 were waited for; matrix products, arithmetic and copies ran while one was open for 0% of the time, Pallas kernels for 13%

profile of v1, /device:TPU:1, one launch (start us, length us, event | category | flops | bytes accessed | tf_op | source)
XLA Modules:
  0.0 132.7 jit_solution(12771141275309226286)
XLA Ops:
  0.0 0.7 copy-done.1
  0.7 2.5 %pack_rows.1 = bf16[1024,128]{1,0:T(8,128)(2,1)} custom-call(bf16[80,768]{1,0:T(8,128)(2,1)} %rows_hbm.1, s32[12,1,128]{2,1,0:T(1,128)S(1)} %bitcast.11), custom_call_target="tpu_custom_call" | custom-call | tf_op jit(solution)/shard_map/pack_rows/pallas_call | solution.py:421
  3.2 11.5 %all-to-all-start = ((bf16[128,8,128]{2,1,0:T(8,128)(2,1)}), bf16[128,8,128]{2,1,0:T(8,128)(2,1)S(1)}, u32[]{:S(2)}, u32[]{:S(2)}) async-start(bf16[128,8,128]{2,1,0:T(8,128)(2,1)} %bitcast.1), calls=%async_computation | async-start | bytes 524288 | tf_op jit(solution)/shard_map/all_to_all | solution.py:408
  14.8 7.4 %bundle.1 = (bf16[6,40,80,128]{3,2,1,0:T(8,128)(2,1)}, bf16[6,40,80,128]{3,2,1,0:T(8,128)(2,1)}, bf16[2,80,80,128]{3,2,1,0:T(8,128)(2,1)S(1)}) custom-call(bf16[6,80,80,128]{3,2,1,0:T(8,128)(2,1)} %coupling_hbm.3, bf16[6,80,80,128]{3,2,1,0:T(8,128)(2,1)} %inverses_hbm.3), custom_call_target="tpu_custom_call" | custom-call | bytes 19660800 | tf_op jit(solution)/shard_map/bundle/pallas_call | solution.py:435
  22.2 3.4 %all-to-all-done = bf16[128,8,128]{2,1,0:T(8,128)(2,1)S(1)} async-done(((bf16[128,8,128]{2,1,0:T(8,128)(2,1)}), bf16[128,8,128]{2,1,0:T(8,128)(2,1)S(1)}, u32[]{:S(2)}, u32[]{:S(2)}) %all-to-all-start) | async-done | bytes 262176 | tf_op jit(solution)/shard_map/all_to_all | solution.py:408
  25.6 4.6 %forcing.1 = (f32[6,40,128]{2,1,0:T(8,128)S(1)}, f32[6,40,128]{2,1,0:T(8,128)S(1)}, bf16[6,40,80,128]{3,2,1,0:T(8,128)(2,1)S(1)}, f32[40,128]{1,0:T(8,128)S(1)}) custom-call(bf16[1024,128]{1,0:T(8,128)(2,1)S(1)} %bitcast.6, s32[12,1,128]{2,1,0:T(1,128)S(1)} %bitcast.9, s32[1,128]{1,0:T(1,128)S(1)} %copy-done.3, ...), custom_call_target="tpu_custom_call" | custom-call | tf_op jit(solution)/shard_map/forcing/pallas_call | solution.py:452
  30.2 1.6 %collective-permute-start = (f32[40,128]{1,0:T(8,128)S(1)}, f32[40,128]{1,0:T(8,128)S(1)}, u32[]{:S(2)}, u32[]{:S(2)}) collective-permute-start(f32[40,128]{1,0:T(8,128)S(1)} %get-tuple-element.22), channel_id=1, source_target_pairs={{0,16},{1,17},{2,18},{3,19},{4,20},{5,21},{6,22},{7,23},{8,24},{9,... | collective-permute-start | bytes 61448 | tf_op jit(solution)/shard_map/ppermute | solution.py:543
  31.8 2.4 %first_hop.1 = (f32[40,128]{1,0:T(8,128)S(1)}, bf16[6,40,80,128]{3,2,1,0:T(8,128)(2,1)S(1)}) custom-call(bf16[6,40,80,128]{3,2,1,0:T(8,128)(2,1)} %get-tuple-element.23.bundle_hbm, f32[6,40,128]{2,1,0:T(8,128)S(1)} %get-tuple-element.24.forcing_ref.refs_9_), custom_call_target="tpu_custom_call" | custom-call | tf_op jit(solution)/shard_map/first_hop/pallas_call | solution.py:469
  34.2 1.3 collective-permute-start.2
  35.5 2.1 %heads.1 = (bf16[1,40,80,128]{3,2,1,0:T(8,128)(2,1)S(1)}, bf16[1,40,80,128]{3,2,1,0:T(8,128)(2,1)S(1)}) custom-call(f32[40,128]{1,0:T(8,128)S(1)} %get-tuple-element.25.after_ref, bf16[6,80,80,128]{3,2,1,0:T(8,128)(2,1)} %coupling_hbm.3), custom_call_target="tpu_custom_call" | custom-call | flops 1000000 | bytes 4000000 | tf_op jit(solution)/shard_map/heads/pallas_call | solution.py:478
  37.7 0.7 collective-permute-start.1
  38.4 0.7 collective-permute-start.16
  39.0 0.8 widen.2.coupling_ref.refs_8_
  39.8 0.8 widen.3.coupling_ref.refs_8_
  40.7 0.7 collective-permute-start.3
  41.4 0.7 collective-permute-start.17
  42.1 0.7 collective-permute-start.4
  42.8 0.7 collective-permute-start.18
  43.5 0.7 collective-permute-start.5
  44.2 0.7 collective-permute-start.19
  44.9 0.7 collective-permute-start.6
  45.6 0.7 collective-permute-start.20
  46.3 0.7 collective-permute-start.7
  47.0 0.7 collective-permute-start.21
  47.7 1.3 collective-permute-start.8
  49.1 1.3 collective-permute-start.22
  50.4 16.5 %collective-permute-done.8.state_ref.refs_0_ = f32[40,128]{1,0:T(8,128)S(1)} collective-permute-done((f32[40,128]{1,0:T(8,128)S(1)}, f32[40,128]{1,0:T(8,128)S(1)}, u32[]{:S(2)}, u32[]{:S(2)}) %collective-permute-start.8) | collective-permute-done | bytes 20512 | tf_op jit(solution)/shard_map/ppermute | solution.py:543
  66.9 0.9 hop_a.21
  67.8 1.3 collective-permute-start.9
  69.6 0.9 hop_b.21
  70.5 1.3 collective-permute-start.23
  71.8 0.7 collective-permute-start.10
  72.7 0.7 collective-permute-start.24
  73.4 0.7 collective-permute-start.11
  74.1 0.7 collective-permute-start.25
  74.8 0.7 collective-permute-start.12
  75.5 0.7 collective-permute-start.26
  76.2 0.7 collective-permute-start.13
  76.9 0.7 collective-permute-start.27
  77.6 0.7 collective-permute-start.14
  78.3 0.7 collective-permute-start.28
  79.0 0.7 collective-permute-start.15
  79.7 0.7 collective-permute-start.29
  81.0 0.9 final_a.1.solved_a
  81.8 0.9 final_b.1.solved_b
  82.7 1.6 %return_pack.1 = s16[1024,128]{1,0:T(8,128)(2,1)S(1)} custom-call(f32[6,40,128]{2,1,0:T(8,128)S(1)} %final_a.1.solved_a, f32[6,40,128]{2,1,0:T(8,128)S(1)} %final_b.1.solved_b, bf16[768,768]{1,0:T(8,128)(2,1)S(1)} %get-tuple-element.33.even_ref, bf16[768,768]{1,0:T(8,128)(2,1)S(1)} %get-tuple-element.34.odd_ref), custom_call_target="tpu_custom_call" | custom-call | tf_op jit(solution)/shard_map/return_pack/pallas_call | solution.py:553
  84.4 45.6 %all_to_all.10 = s16[128,8,128]{2,1,0:T(8,128)(2,1)S(1)} all-to-all(s16[128,8,128]{2,1,0:T(8,128)(2,1)S(1)} %bitcast.8), channel_id=1, replica_groups=mesh['circ'=8,'span'=16] {'circ','span'}, dimensions={0} | all-to-all | bytes 524288 | tf_op jit(solution)/shard_map/all_to_all | solution.py:408
  130.0 2.7 %return_rows.1 = f32[80,768]{1,0:T(8,128)} custom-call(s16[1024,128]{1,0:T(8,128)(2,1)S(1)} %bitcast.7, s32[12,1,128]{2,1,0:T(1,128)S(1)} %bitcast.12), custom_call_target="tpu_custom_call" | custom-call | tf_op jit(solution)/shard_map/return_rows/pallas_call | solution.py:563
  (63 shorter events, 1.8 us)
Async XLA Ops:
  0.0 0.7 copy-start.1
  3.2 22.3 %all-to-all-start = ((bf16[128,8,128]{2,1,0:T(8,128)(2,1)}), bf16[128,8,128]{2,1,0:T(8,128)(2,1)S(1)}, u32[]{:S(2)}, u32[]{:S(2)}) async-start(bf16[128,8,128]{2,1,0:T(8,128)(2,1)} %bitcast.1), calls=%async_computation | async-start | bytes 524288 | tf_op jit(solution)/shard_map/all_to_all | solution.py:408
  14.7 10.8 %copy-start = (s32[1,128,12]{1,0,2:T(1,128)S(1)}, s32[1,128,12]{1,0,2:T(1,128)}, u32[]{:S(2)}) copy-start(s32[1,128,12]{1,0,2:T(1,128)} %param.10) | copy-start | bytes 18436
  14.7 10.8 %copy-start.3 = (s32[1,128]{1,0:T(1,128)S(1)}, s32[1,128]{1,0:T(1,128)}, u32[]{:S(2)}) copy-start(s32[1,128]{1,0:T(1,128)} %counts_ref.2) | copy-start | bytes 1540
  30.2 7.5 %collective-permute-start = (f32[40,128]{1,0:T(8,128)S(1)}, f32[40,128]{1,0:T(8,128)S(1)}, u32[]{:S(2)}, u32[]{:S(2)}) collective-permute-start(f32[40,128]{1,0:T(8,128)S(1)} %get-tuple-element.22), channel_id=1, source_target_pairs={{0,16},{1,17},{2,18},{3,19},{4,20},{5,21},{6,22},{7,23},{8,24},{9,... | collective-permute-start | bytes 61448 | tf_op jit(solution)/shard_map/ppermute | solution.py:543
  34.2 4.1 %collective-permute-start.2 = (f32[40,128]{1,0:T(8,128)S(1)}, f32[40,128]{1,0:T(8,128)S(1)}, u32[]{:S(2)}, u32[]{:S(2)}) collective-permute-start(f32[40,128]{1,0:T(8,128)S(1)} %get-tuple-element.25.after_ref), channel_id=1, source_target_pairs={{0,16},{1,17},{2,18},{3,19},{4,20},{5,21},{6,22},{7,23},{8,24},{9,... | collective-permute-start | bytes 61448 | tf_op jit(solution)/shard_map/ppermute | solution.py:543
  37.7 3.0 %collective-permute-start.1 = (f32[40,128]{1,0:T(8,128)S(1)}, f32[40,128]{1,0:T(8,128)S(1)}, u32[]{:S(2)}, u32[]{:S(2)}) collective-permute-start(f32[40,128]{1,0:T(8,128)S(1)} %hop_a.14), channel_id=1, source_target_pairs={{16,32},{17,33},{18,34},{19,35},{20,36},{21,37},{22,38},{23,39},{2... | collective-permute-start | bytes 61448 | tf_op jit(solution)/shard_map/ppermute | solution.py:543
  38.4 3.0 %collective-permute-start.16 = (f32[40,128]{1,0:T(8,128)S(1)}, f32[40,128]{1,0:T(8,128)S(1)}, u32[]{:S(2)}, u32[]{:S(2)}) collective-permute-start(f32[40,128]{1,0:T(8,128)S(1)} %hop_b.14.after_ref), channel_id=1, source_target_pairs={{16,32},{17,33},{18,34},{19,35},{20,36},{21,37},{22,38},{23,39},{2... | collective-permute-start | bytes 61448 | tf_op jit(solution)/shard_map/ppermute | solution.py:543
  40.7 1.4 %collective-permute-start.3 = (f32[40,128]{1,0:T(8,128)S(1)}, f32[40,128]{1,0:T(8,128)S(1)}, u32[]{:S(2)}, u32[]{:S(2)}) collective-permute-start(f32[40,128]{1,0:T(8,128)S(1)} %hop_a.15), channel_id=1, source_target_pairs={{32,48},{33,49},{34,50},{35,51},{36,52},{37,53},{38,54},{39,55},{4... | collective-permute-start | bytes 61448 | tf_op jit(solution)/shard_map/ppermute | solution.py:543
  41.4 1.4 %collective-permute-start.17 = (f32[40,128]{1,0:T(8,128)S(1)}, f32[40,128]{1,0:T(8,128)S(1)}, u32[]{:S(2)}, u32[]{:S(2)}) collective-permute-start(f32[40,128]{1,0:T(8,128)S(1)} %hop_b.15), channel_id=1, source_target_pairs={{32,48},{33,49},{34,50},{35,51},{36,52},{37,53},{38,54},{39,55},{4... | collective-permute-start | bytes 61448 | tf_op jit(solution)/shard_map/ppermute | solution.py:543
  42.1 1.4 %collective-permute-start.4 = (f32[40,128]{1,0:T(8,128)S(1)}, f32[40,128]{1,0:T(8,128)S(1)}, u32[]{:S(2)}, u32[]{:S(2)}) collective-permute-start(f32[40,128]{1,0:T(8,128)S(1)} %hop_a.16), channel_id=1, source_target_pairs={{48,64},{49,65},{50,66},{51,67},{52,68},{53,69},{54,70},{55,71},{5... | collective-permute-start | bytes 61448 | tf_op jit(solution)/shard_map/ppermute | solution.py:543
  42.8 1.4 %collective-permute-start.18 = (f32[40,128]{1,0:T(8,128)S(1)}, f32[40,128]{1,0:T(8,128)S(1)}, u32[]{:S(2)}, u32[]{:S(2)}) collective-permute-start(f32[40,128]{1,0:T(8,128)S(1)} %hop_b.16), channel_id=1, source_target_pairs={{48,64},{49,65},{50,66},{51,67},{52,68},{53,69},{54,70},{55,71},{5... | collective-permute-start | bytes 61448 | tf_op jit(solution)/shard_map/ppermute | solution.py:543
  43.5 1.4 %collective-permute-start.5 = (f32[40,128]{1,0:T(8,128)S(1)}, f32[40,128]{1,0:T(8,128)S(1)}, u32[]{:S(2)}, u32[]{:S(2)}) collective-permute-start(f32[40,128]{1,0:T(8,128)S(1)} %hop_a.17), channel_id=1, source_target_pairs={{64,80},{65,81},{66,82},{67,83},{68,84},{69,85},{70,86},{71,87},{7... | collective-permute-start | bytes 61448 | tf_op jit(solution)/shard_map/ppermute | solution.py:543
  44.2 1.4 %collective-permute-start.19 = (f32[40,128]{1,0:T(8,128)S(1)}, f32[40,128]{1,0:T(8,128)S(1)}, u32[]{:S(2)}, u32[]{:S(2)}) collective-permute-start(f32[40,128]{1,0:T(8,128)S(1)} %hop_b.17), channel_id=1, source_target_pairs={{64,80},{65,81},{66,82},{67,83},{68,84},{69,85},{70,86},{71,87},{7... | collective-permute-start | bytes 61448 | tf_op jit(solution)/shard_map/ppermute | solution.py:543
  44.9 1.4 %collective-permute-start.6 = (f32[40,128]{1,0:T(8,128)S(1)}, f32[40,128]{1,0:T(8,128)S(1)}, u32[]{:S(2)}, u32[]{:S(2)}) collective-permute-start(f32[40,128]{1,0:T(8,128)S(1)} %hop_a.18), channel_id=1, source_target_pairs={{80,96},{81,97},{82,98},{83,99},{84,100},{85,101},{86,102},{87,103... | collective-permute-start | bytes 61448 | tf_op jit(solution)/shard_map/ppermute | solution.py:543
  45.6 1.4 %collective-permute-start.20 = (f32[40,128]{1,0:T(8,128)S(1)}, f32[40,128]{1,0:T(8,128)S(1)}, u32[]{:S(2)}, u32[]{:S(2)}) collective-permute-start(f32[40,128]{1,0:T(8,128)S(1)} %hop_b.18), channel_id=1, source_target_pairs={{80,96},{81,97},{82,98},{83,99},{84,100},{85,101},{86,102},{87,103... | collective-permute-start | bytes 61448 | tf_op jit(solution)/shard_map/ppermute | solution.py:543
  46.3 1.4 %collective-permute-start.7 = (f32[40,128]{1,0:T(8,128)S(1)}, f32[40,128]{1,0:T(8,128)S(1)}, u32[]{:S(2)}, u32[]{:S(2)}) collective-permute-start(f32[40,128]{1,0:T(8,128)S(1)} %hop_a.19), channel_id=1, source_target_pairs={{96,112},{97,113},{98,114},{99,115},{100,116},{101,117},{102,118},... | collective-permute-start | bytes 61448 | tf_op jit(solution)/shard_map/ppermute | solution.py:543
  47.0 2.0 %collective-permute-start.21 = (f32[40,128]{1,0:T(8,128)S(1)}, f32[40,128]{1,0:T(8,128)S(1)}, u32[]{:S(2)}, u32[]{:S(2)}) collective-permute-start(f32[40,128]{1,0:T(8,128)S(1)} %hop_b.19), channel_id=1, source_target_pairs={{96,112},{97,113},{98,114},{99,115},{100,116},{101,117},{102,118},... | collective-permute-start | bytes 61448 | tf_op jit(solution)/shard_map/ppermute | solution.py:543
  47.7 19.2 %collective-permute-start.8 = (f32[40,128]{1,0:T(8,128)S(1)}, f32[40,128]{1,0:T(8,128)S(1)}, u32[]{:S(2)}, u32[]{:S(2)}) collective-permute-start(f32[40,128]{1,0:T(8,128)S(1)} %hop_a.20), channel_id=1, source_target_pairs={{112,0},{113,1},{114,2},{115,3},{116,4},{117,5},{118,6},{119,7},{1... | collective-permute-start | bytes 61448 | tf_op jit(solution)/shard_map/ppermute | solution.py:543
  49.1 20.6 %collective-permute-start.22 = (f32[40,128]{1,0:T(8,128)S(1)}, f32[40,128]{1,0:T(8,128)S(1)}, u32[]{:S(2)}, u32[]{:S(2)}) collective-permute-start(f32[40,128]{1,0:T(8,128)S(1)} %hop_b.20), channel_id=1, source_target_pairs={{112,0},{113,1},{114,2},{115,3},{116,4},{117,5},{118,6},{119,7},{1... | collective-permute-start | bytes 61448 | tf_op jit(solution)/shard_map/ppermute | solution.py:543
  67.8 4.0 %collective-permute-start.9 = (f32[40,128]{1,0:T(8,128)S(1)}, f32[40,128]{1,0:T(8,128)S(1)}, u32[]{:S(2)}, u32[]{:S(2)}) collective-permute-start(f32[40,128]{1,0:T(8,128)S(1)} %hop_a.21), channel_id=1, source_target_pairs={{0,16},{1,17},{2,18},{3,19},{4,20},{5,21},{6,22},{7,23},{8,24},{9,... | collective-permute-start | bytes 61448 | tf_op jit(solution)/shard_map/ppermute | solution.py:543
  70.5 2.2 %collective-permute-start.23 = (f32[40,128]{1,0:T(8,128)S(1)}, f32[40,128]{1,0:T(8,128)S(1)}, u32[]{:S(2)}, u32[]{:S(2)}) collective-permute-start(f32[40,128]{1,0:T(8,128)S(1)} %hop_b.21), channel_id=1, source_target_pairs={{0,16},{1,17},{2,18},{3,19},{4,20},{5,21},{6,22},{7,23},{8,24},{9,... | collective-permute-start | bytes 61448 | tf_op jit(solution)/shard_map/ppermute | solution.py:543
  71.8 1.5 %collective-permute-start.10 = (f32[40,128]{1,0:T(8,128)S(1)}, f32[40,128]{1,0:T(8,128)S(1)}, u32[]{:S(2)}, u32[]{:S(2)}) collective-permute-start(f32[40,128]{1,0:T(8,128)S(1)} %hop_a.22), channel_id=1, source_target_pairs={{16,32},{17,33},{18,34},{19,35},{20,36},{21,37},{22,38},{23,39},{2... | collective-permute-start | bytes 61448 | tf_op jit(solution)/shard_map/ppermute | solution.py:543
  72.7 1.4 %collective-permute-start.24 = (f32[40,128]{1,0:T(8,128)S(1)}, f32[40,128]{1,0:T(8,128)S(1)}, u32[]{:S(2)}, u32[]{:S(2)}) collective-permute-start(f32[40,128]{1,0:T(8,128)S(1)} %hop_b.22), channel_id=1, source_target_pairs={{16,32},{17,33},{18,34},{19,35},{20,36},{21,37},{22,38},{23,39},{2... | collective-permute-start | bytes 61448 | tf_op jit(solution)/shard_map/ppermute | solution.py:543
  73.4 1.4 %collective-permute-start.11 = (f32[40,128]{1,0:T(8,128)S(1)}, f32[40,128]{1,0:T(8,128)S(1)}, u32[]{:S(2)}, u32[]{:S(2)}) collective-permute-start(f32[40,128]{1,0:T(8,128)S(1)} %hop_a.23), channel_id=1, source_target_pairs={{32,48},{33,49},{34,50},{35,51},{36,52},{37,53},{38,54},{39,55},{4... | collective-permute-start | bytes 61448 | tf_op jit(solution)/shard_map/ppermute | solution.py:543
  74.1 1.4 %collective-permute-start.25 = (f32[40,128]{1,0:T(8,128)S(1)}, f32[40,128]{1,0:T(8,128)S(1)}, u32[]{:S(2)}, u32[]{:S(2)}) collective-permute-start(f32[40,128]{1,0:T(8,128)S(1)} %hop_b.23), channel_id=1, source_target_pairs={{32,48},{33,49},{34,50},{35,51},{36,52},{37,53},{38,54},{39,55},{4... | collective-permute-start | bytes 61448 | tf_op jit(solution)/shard_map/ppermute | solution.py:543
  74.8 1.4 %collective-permute-start.12 = (f32[40,128]{1,0:T(8,128)S(1)}, f32[40,128]{1,0:T(8,128)S(1)}, u32[]{:S(2)}, u32[]{:S(2)}) collective-permute-start(f32[40,128]{1,0:T(8,128)S(1)} %hop_a.24), channel_id=1, source_target_pairs={{48,64},{49,65},{50,66},{51,67},{52,68},{53,69},{54,70},{55,71},{5... | collective-permute-start | bytes 61448 | tf_op jit(solution)/shard_map/ppermute | solution.py:543
  75.5 1.4 %collective-permute-start.26 = (f32[40,128]{1,0:T(8,128)S(1)}, f32[40,128]{1,0:T(8,128)S(1)}, u32[]{:S(2)}, u32[]{:S(2)}) collective-permute-start(f32[40,128]{1,0:T(8,128)S(1)} %hop_b.24), channel_id=1, source_target_pairs={{48,64},{49,65},{50,66},{51,67},{52,68},{53,69},{54,70},{55,71},{5... | collective-permute-start | bytes 61448 | tf_op jit(solution)/shard_map/ppermute | solution.py:543
  76.2 1.4 %collective-permute-start.13 = (f32[40,128]{1,0:T(8,128)S(1)}, f32[40,128]{1,0:T(8,128)S(1)}, u32[]{:S(2)}, u32[]{:S(2)}) collective-permute-start(f32[40,128]{1,0:T(8,128)S(1)} %hop_a.25), channel_id=1, source_target_pairs={{64,80},{65,81},{66,82},{67,83},{68,84},{69,85},{70,86},{71,87},{7... | collective-permute-start | bytes 61448 | tf_op jit(solution)/shard_map/ppermute | solution.py:543
  76.9 1.4 %collective-permute-start.27 = (f32[40,128]{1,0:T(8,128)S(1)}, f32[40,128]{1,0:T(8,128)S(1)}, u32[]{:S(2)}, u32[]{:S(2)}) collective-permute-start(f32[40,128]{1,0:T(8,128)S(1)} %hop_b.25), channel_id=1, source_target_pairs={{64,80},{65,81},{66,82},{67,83},{68,84},{69,85},{70,86},{71,87},{7... | collective-permute-start | bytes 61448 | tf_op jit(solution)/shard_map/ppermute | solution.py:543
  77.6 1.4 %collective-permute-start.14 = (f32[40,128]{1,0:T(8,128)S(1)}, f32[40,128]{1,0:T(8,128)S(1)}, u32[]{:S(2)}, u32[]{:S(2)}) collective-permute-start(f32[40,128]{1,0:T(8,128)S(1)} %hop_a.26), channel_id=1, source_target_pairs={{80,96},{81,97},{82,98},{83,99},{84,100},{85,101},{86,102},{87,103... | collective-permute-start | bytes 61448 | tf_op jit(solution)/shard_map/ppermute | solution.py:543
  78.3 1.4 %collective-permute-start.28 = (f32[40,128]{1,0:T(8,128)S(1)}, f32[40,128]{1,0:T(8,128)S(1)}, u32[]{:S(2)}, u32[]{:S(2)}) collective-permute-start(f32[40,128]{1,0:T(8,128)S(1)} %hop_b.26), channel_id=1, source_target_pairs={{80,96},{81,97},{82,98},{83,99},{84,100},{85,101},{86,102},{87,103... | collective-permute-start | bytes 61448 | tf_op jit(solution)/shard_map/ppermute | solution.py:543
  79.0 1.9 %collective-permute-start.15 = (f32[40,128]{1,0:T(8,128)S(1)}, f32[40,128]{1,0:T(8,128)S(1)}, u32[]{:S(2)}, u32[]{:S(2)}) collective-permute-start(f32[40,128]{1,0:T(8,128)S(1)} %hop_a.27), channel_id=1, source_target_pairs={{96,112},{97,113},{98,114},{99,115},{100,116},{101,117},{102,118},... | collective-permute-start | bytes 61448 | tf_op jit(solution)/shard_map/ppermute | solution.py:543
  79.7 2.1 %collective-permute-start.29 = (f32[40,128]{1,0:T(8,128)S(1)}, f32[40,128]{1,0:T(8,128)S(1)}, u32[]{:S(2)}, u32[]{:S(2)}) collective-permute-start(f32[40,128]{1,0:T(8,128)S(1)} %hop_b.27), channel_id=1, source_target_pairs={{96,112},{97,113},{98,114},{99,115},{100,116},{101,117},{102,118},... | collective-permute-start | bytes 61448 | tf_op jit(solution)/shard_map/ppermute | solution.py:543
  81.8 48.2 %copy-start.2 = (s32[1,128,12]{1,0,2:T(1,128)S(1)}, s32[1,128,12]{1,0,2:T(1,128)}, u32[]{:S(2)}) copy-start(s32[1,128,12]{1,0,2:T(1,128)} %param.9) | copy-start | bytes 18436
